TPU v7x, 32 devices: a whole 2x2x4 slice. The times are simulated.
32 devices in a mesh: freq: 8 (over z, x), bl: 4 (over y, core).
Axes of the slice: x: 2, y: 2, z: 4, core: 2. Of those that a mesh axis runs over, the one named last changes fastest.
Arguments:
- voltages: bfloat16 [1024, 134144], P(('bl', 'freq')), may hold values from -6 to 6
- fir_taps: float32 [4, 1024], replicated, may hold values from -3 to 3
- antenna_order: int32 [1024], replicated, may hold values from 0 to 1023, each once
- tile_list: int32 [4, 2], replicated, may hold values from 0 to 3
Outputs:
- visibilities: bfloat16 [4, 512, 256, 512], P('bl', 'freq')
All inputs are finite; a program needn't handle non-finite values.
Results may differ from a plain program's by a relative error of at most 0.0074.
Values may be sent and summed in bfloat16 or wider, within the bound.
A program may use at most 128 MiB of HBM per device.

v0:
```python
import math
import jax
import jax.numpy as jnp
from jax import lax
from jax.sharding import PartitionSpec as P

K = 1024
TAPS = 4
PANEL = 256
SAMPLES = 128


def make_table(points, kept):
    product = (
        jnp.arange(points, dtype=jnp.int32)[:, None]
        * jnp.arange(kept, dtype=jnp.int32)[None, :]
        % points
    )
    phase = 2.0 * math.pi / points * product.astype(jnp.float32)
    return jnp.concatenate([jnp.cos(phase), -jnp.sin(phase)], axis=1).astype(jnp.bfloat16)


def arrange(panel):
    width = panel.shape[1]
    return jnp.transpose(panel, (3, 0, 2, 1)).reshape(panel.shape[3], panel.shape[0], 2 * width)


def rotated(panel):
    turned = jnp.stack([-panel[:, :, 1, :], panel[:, :, 0, :]], axis=2)
    return arrange(turned)


def correlate(source, antenna_order, tile):
    row_ids = lax.dynamic_slice_in_dim(antenna_order, tile[0] * PANEL, PANEL)
    col_ids = lax.dynamic_slice_in_dim(antenna_order, tile[1] * PANEL, PANEL)
    row_panel = jnp.take(source, row_ids, axis=0)
    col_panel = jnp.take(source, col_ids, axis=0)
    left = arrange(row_panel)
    right = jnp.concatenate([arrange(col_panel), rotated(col_panel)], axis=1)
    return jnp.einsum("fps,fqs->fpq", left, right, preferred_element_type=jnp.float32)


def per_device(voltages, fir_taps, antenna_order, tile_list):
    local_count = voltages.shape[0]
    frames = voltages.reshape(local_count, SAMPLES + TAPS - 1, K)
    filtered = jnp.zeros((local_count, SAMPLES, K), jnp.float32)
    for tap in range(TAPS):
        filtered = filtered + fir_taps[tap][None, None, :] * frames[
            :, tap : tap + SAMPLES, :
        ].astype(jnp.float32)
    filtered = filtered.astype(jnp.bfloat16)
    table = make_table(K, K // 2)
    spectra = jnp.dot(
        filtered.reshape(local_count * SAMPLES, K), table, preferred_element_type=jnp.float32
    )
    spectra = (
        (spectra * (1.0 / math.sqrt(K)))
        .astype(jnp.bfloat16)
        .reshape(local_count, SAMPLES, 2, K // 2)
    )
    turned = lax.all_to_all(spectra, "freq", split_axis=3, concat_axis=0, tiled=True)
    gathered = lax.all_gather(turned, "bl", axis=0, tiled=True)
    own_tile = tile_list[lax.axis_index("bl")]
    summed = correlate(gathered, antenna_order, own_tile)
    return (summed / SAMPLES).astype(jnp.bfloat16)[None]


def solution(mesh):
    return jax.shard_map(
        per_device,
        mesh=mesh,
        in_specs=(P(("bl", "freq"), None), P(), P(), P()),
        out_specs=P("bl", "freq", None, None),
        check_vma=False,
    )
```

profile of v0, /device:TPU:0, one launch (start us, length us, event | category | flops | bytes accessed | tf_op | source)
XLA Modules:
  0.0 656.6 jit_solution(10840728497448380260)
XLA Ops:
  6.5 8.5 %negate_convert_fusion = (bf16[1024,512]{1,0:T(8,128)(2,1)S(1)}, bf16[1024,512]{1,0:T(8,128)(2,1)S(1)}) fusion(), kind=kLoop, calls=%fused_computation.23 | loop fusion | flops 8912896 | bytes 2097152 | tf_op jit(solution)/shard_map/convert.1
  15.1 9.2 %reshape.35 = bf16[32,131,1024]{2,1,0:T(8,128)(2,1)} reshape(bf16[32,134144]{1,0:T(8,128)(2,1)} %param.6) | data formatting | bytes 17170432 | tf_op jit(solution)/shard_map/reshape | solution.py:45
  24.3 19.3 %add_convert_fusion = bf16[32,128,1024]{2,1,0:T(8,128)(2,1)S(1)} fusion(bf16[32,131,1024]{2,1,0:T(8,128)(2,1)} %reshape.35, f32[1024]{0:T(1024)S(1)} %bitcast.28, f32[1024]{0:T(1024)S(1)} %bitcast.29, f32[1024]{0:T(1024)S(1)} %bitcast.27, f32[1024]{0:T(1024)S(1)} %bitcast.26), kind=kLoop, calls=%fused_computation.9 | loop fusion | flops 50331648 | bytes 41959424 | tf_op jit(solution)/shard_map/convert_element_type | solution.py:51
  43.6 11.0 %multiply_convert_fusion.1 = bf16[4096,1024]{1,0:T(8,128)(2,1)} fusion(bf16[4096,1024]{1,0:T(8,128)(2,1)S(1)} %bitcast.24, bf16[1024,512]{1,0:T(8,128)(2,1)S(1)} %get-tuple-element.20, bf16[1024,512]{1,0:T(8,128)(2,1)S(1)} %get-tuple-element.21), kind=kOutput, calls=%fused_computation.8 | convolution fusion | flops 8602517504 | bytes 18874368 | tf_op jit(solution)/shard_map/dot_general | solution.py:53
  54.6 14.5 %reshape.37 = bf16[32,128,2,512]{3,2,1,0:T(2,128)(2,1)} reshape(bf16[4096,1024]{1,0:T(8,128)(2,1)} %multiply_convert_fusion.1) | data formatting | bytes 16777216 | tf_op jit(solution)/shard_map/reshape | solution.py:59
  69.1 28.1 %copy.15 = bf16[32,128,2,512]{1,2,0,3:T(2,128)(2,1)} copy(bf16[32,128,2,512]{3,2,1,0:T(2,128)(2,1)} %reshape.37) | data formatting | bytes 16777216 | tf_op jit(solution)/shard_map/reshape | solution.py:59
  97.2 190.4 %all_to_all.18 = bf16[32,128,2,512]{1,2,0,3:T(2,128)(2,1)} all-to-all(bf16[32,128,2,512]{1,2,0,3:T(2,128)(2,1)} %copy.15), channel_id=1, replica_groups=mesh['freq'=8,'bl'=4] {'freq'}, dimensions={3} | all-to-all | bytes 16777216 | tf_op jit(solution)/shard_map/all_to_all | solution.py:61
  287.6 16.5 %copy.16 = bf16[32,128,2,512]{1,3,2,0:T(8,128)(2,1)} copy(bf16[32,128,2,512]{1,2,0,3:T(2,128)(2,1)} %all_to_all.18) | data formatting | bytes 16777216 | tf_op jit(solution)/shard_map/all_to_all | solution.py:61
  304.1 9.8 %copy.17 = bf16[8,32,128,2,64]{2,4,3,1,0:T(8,128)(2,1)} copy(bf16[8,32,128,2,64]{2,4,0,3,1:T(8,128)(2,1)} %bitcast.23) | data formatting | bytes 16777216 | tf_op jit(solution)/shard_map/all_to_all | solution.py:61
  314.0 0.5 fusion.19
  315.9 198.8 %all-gather.2.cloned.1.call-done = bf16[1024,128,2,64]{1,3,2,0:T(8,128)(2,1)} async-done(((bf16[256,128,2,64]{1,3,2,0:T(8,128)(2,1)}), bf16[1024,128,2,64]{1,3,2,0:T(8,128)(2,1)}) %all-gather.2.cloned.1.call-update) | async-done | bytes 33554448 | tf_op jit(solution)/shard_map/all_gather | solution.py:62
  514.7 9.1 %gather_fusion.1 = bf16[256,128,2,64]{1,3,2,0:T(8,128)(2,1)} fusion(bf16[1024,128,2,64]{1,3,2,0:T(8,128)(2,1)} %all-gather.2.cloned.1.call-done, s32[1024]{0:T(1024)S(1)} %get-tuple-element.22), kind=kCustom, calls=%fused_computation.1.clone | custom fusion | bytes 16778240 | tf_op jit(solution)/shard_map/jit(_take)/gather | solution.py:37
  523.8 7.4 %broadcast_select_fusion = bf16[256,128,2,64]{1,3,2,0:T(8,128)(2,1)} fusion(bf16[256,128,2,64]{1,3,2,0:T(8,128)(2,1)} %gather_fusion.1, pred[256]{0:T(512)(128)(4,1)S(1)} %get-tuple-element.6), kind=kLoop, calls=%fused_computation.12 | loop fusion | flops 4194304 | bytes 16777472 | tf_op jit(solution)/shard_map/jit(_take)/select_n | solution.py:37
  531.3 7.4 %fusion.22 = bf16[64,256,2,128]{3,0,2,1:T(8,128)(2,1)} fusion(bf16[256,128,2,64]{1,3,2,0:T(8,128)(2,1)} %gather_fusion.1, pred[256]{0:T(512)(128)(4,1)S(1)} %get-tuple-element.6), kind=kLoop, calls=%fused_computation.39 | loop fusion | flops 4194304 | bytes 16777472 | tf_op jit(solution)/shard_map/transpose | solution.py:25
  538.7 9.1 %gather_fusion = bf16[256,128,2,64]{1,3,2,0:T(8,128)(2,1)} fusion(bf16[1024,128,2,64]{1,3,2,0:T(8,128)(2,1)} %all-gather.2.cloned.1.call-done, s32[1024]{0:T(1024)S(1)} %get-tuple-element.23), kind=kCustom, calls=%fused_computation.clone | custom fusion | bytes 16778240 | tf_op jit(solution)/shard_map/jit(_take)/gather | solution.py:36
  547.8 7.6 %select_bitcast_fusion = bf16[64,256,2,128]{3,0,2,1:T(8,128)(2,1)} fusion(bf16[256,128,2,64]{1,3,2,0:T(8,128)(2,1)} %gather_fusion, pred[256]{0:T(512)(128)(4,1)S(1)} %get-tuple-element.16), kind=kLoop, calls=%fused_computation.11 | loop fusion | flops 4194304 | bytes 16777472 | tf_op jit(solution)/shard_map/transpose | solution.py:25
  555.4 12.9 %copy.18 = bf16[64,256,2,128]{1,3,2,0:T(8,128)(2,1)} copy(bf16[64,256,2,128]{3,0,2,1:T(8,128)(2,1)} %select_bitcast_fusion) | data formatting | bytes 16777216 | tf_op jit(solution)/shard_map/transpose | solution.py:25
  568.3 5.2 slice_negate_fusion
  573.6 6.5 maximum_bitcast_fusion
  580.0 13.2 %copy.20 = bf16[64,256,2,128]{3,2,1,0:T(2,128)(2,1)} copy(bf16[64,256,2,128]{3,0,2,1:T(8,128)(2,1)} %maximum_bitcast_fusion) | data formatting | bytes 16777216 | tf_op jit(solution)/shard_map/transpose | solution.py:25
  593.2 14.1 %reshape.40 = bf16[64,256,256]{2,1,0:T(8,128)(2,1)} reshape(bf16[64,256,2,128]{3,2,1,0:T(2,128)(2,1)} %copy.20) | data formatting | bytes 16777216 | tf_op jit(solution)/shard_map/reshape | solution.py:25
  607.3 13.2 %copy.19 = bf16[64,256,2,128]{3,2,1,0:T(2,128)(2,1)} copy(bf16[64,256,2,128]{3,0,2,1:T(8,128)(2,1)} %fusion.22) | data formatting | bytes 16777216 | tf_op jit(solution)/shard_map/transpose | solution.py:25
  620.4 14.1 %reshape.39 = bf16[64,256,256]{2,1,0:T(8,128)(2,1)} reshape(bf16[64,256,2,128]{3,2,1,0:T(2,128)(2,1)} %copy.19) | data formatting | bytes 16777216 | tf_op jit(solution)/shard_map/reshape | solution.py:25
  634.5 15.2 %fusion = bf16[1,64,256,512]{3,2,1,0:T(8,128)(2,1)} fusion(bf16[64,256,256]{1,2,0:T(8,128)(2,1)} %bitcast.25, bf16[64,256,256]{2,1,0:T(8,128)(2,1)} %reshape.40, bf16[64,256,256]{2,1,0:T(8,128)(2,1)} %reshape.39), kind=kOutput, calls=%fused_computation.3 | convolution fusion | flops 4345298944 | bytes 41943040 | tf_op jit(solution)/shard_map/fps,fqs->fpq/dot_general | solution.py:40
  (14 shorter events, 0.2 us)
Async XLA Ops:
  6.5 307.4 %copy-start = (s32[4,2]{0,1:T(2,128)S(1)}, s32[4,2]{0,1:T(2,128)}, u32[]{:S(2)}) copy-start(s32[4,2]{0,1:T(2,128)} %param.9) | copy-start | bytes 100
  6.5 508.2 %all-gather.2.cloned.1.call-start = ((), (), s32[]{:S(2)}) async-start(), calls=%async_computation.1 | async-start | bytes 41943040 | tf_op jit(solution)/shard_map/all_gather | solution.py:62
  15.1 9.2 %copy-start.2 = (f32[4,1024]{1,0:T(4,128)S(1)}, f32[4,1024]{1,0:T(4,128)}, u32[]{:S(2)}) copy-start(f32[4,1024]{1,0:T(4,128)} %param.7) | copy-start | bytes 49156
  313.9 1.9 copy-start.3
  634.5 15.2 %copy-start.1 = (s32[4,2]{0,1:T(2,128)S(1)}, s32[4,2]{0,1:T(2,128)}, u32[]{:S(2)}) copy-start(s32[4,2]{0,1:T(2,128)} %param.9) | copy-start | bytes 100
Sparse Core Ops, SparseCore 0:
  314.0 200.6 all-gather.1
where the time goes:
time: 659 us; the launch traced here: 657 us
  waiting for transfers between devices  199 us (30%)
  blocking collectives  190 us (29%)
  local copies, waits for them, and re-layouts  164 us (25%)
  other arithmetic  62.1 us (9%)
  matrix products  26.2 us (4%)
  between operations  14.7 us (2%)
    all_gather x1, waiting for transfers between devices, per_device(): gathered = lax.all_gather(turned, 'bl', axis=0, tiled=True)  199 us
    all_to_all x1, blocking collectives, per_device(): lax.all_to_all(spectra, 'freq', split_axis=3, concat_axis=0, tiled=True)  190 us
    reshape x2, local copies, waits for them, and re-layouts, per_device(): spectra = (spectra * (1.0 / math.sqrt(K))).astype(jnp.bfloat16).reshape(l...  42.6 us
    transpose x3, local copies, waits for them, and re-layouts, arrange(): jnp.transpose(panel, (3, 0, 2, 1))  39.3 us
    reshape x2, local copies, waits for them, and re-layouts, arrange(): jnp.transpose(panel, (3, 0, 2, 1))  28.2 us
    all_to_all x2, local copies, waits for them, and re-layouts, per_device(): lax.all_to_all(spectra, 'freq', split_axis=3, concat_axis=0, tiled=True)  26.3 us
    transpose x3, other arithmetic, arrange(): jnp.transpose(panel, (3, 0, 2, 1))  21.5 us
    convert_element_type x1, other arithmetic, per_device(): filtered = filtered.astype(jnp.bfloat16)  19.3 us
  transfers between devices with their start and end apart: 1, of which 1 were waited for; matrix products, arithmetic and copies ran while one was open for 0% of the time, Pallas kernels for 0%

commit v1 on v0

--- a/solution.py
+++ b/solution.py
@@ -8,6 +8,17 @@
 TAPS = 4
 PANEL = 256
 SAMPLES = 128
+
+
+def cut_along(shard, dim, devices):
+    before, after = (shard.shape[:dim], shard.shape[dim + 1 :])
+    return jnp.moveaxis(shard.reshape(*before, devices, -1, *after), dim, 0)
+
+
+def in_order(parts, dim):
+    parts = jnp.moveaxis(parts, 0, dim)
+    lengths = parts.shape
+    return parts.reshape(*lengths[:dim], lengths[dim] * lengths[dim + 1], *lengths[dim + 2 :])
 
 
 def make_table(points, kept):
@@ -58,7 +69,14 @@
         .astype(jnp.bfloat16)
         .reshape(local_count, SAMPLES, 2, K // 2)
     )
-    turned = lax.all_to_all(spectra, "freq", split_axis=3, concat_axis=0, tiled=True)
+    size, here = (lax.axis_size("freq"), lax.axis_index("freq"))
+    blocks = cut_along(spectra, 3, size)
+    gathered_2 = [blocks[here]]
+    for turn in range(1, size):
+        sent = blocks[here ^ turn]
+        gathered_2.append(lax.ppermute(sent, "freq", [(i, i ^ turn) for i in range(size)]))
+    blocks = jnp.stack(gathered_2)[here ^ jnp.arange(size)]
+    turned = in_order(blocks, 0)
     gathered = lax.all_gather(turned, "bl", axis=0, tiled=True)
     own_tile = tile_list[lax.axis_index("bl")]
     summed = correlate(gathered, antenna_order, own_tile)

time: 659 us -> 625 us (0.948)
  blocking collectives: 190 us -> 0 us
  waiting for transfers between devices: 199 us -> 365 us
  local copies, waits for them, and re-layouts: 164 us -> 141 us
  starting transfers between devices: 0.01 us -> 13.5 us
    all_to_all x1 -> x0, blocking collectives: 190 us -> none  [per_device(): lax.all_to_all(spectra, 'freq', split_axis=3, concat_axis=0, tiled=True)]
    ppermute x0 -> x7, waiting for transfers between devices: none -> 125 us  [per_device(): lax.ppermute(sent, 'freq', [(i, i ^ turn) for i in range(size)])]
    reshape x2 -> x0, local copies, waits for them, and re-layouts: 42.6 us -> none  [per_device(): spectra = (spectra * (1.0 / math.sqrt(K))).astype(jnp.bfloat16).reshape(l...]
    all_gather x1, waiting for transfers between devices: 199 us -> 240 us  [per_device(): gathered = lax.all_gather(turned, 'bl', axis=0, tiled=True)]
    all_to_all x2 -> x0, local copies, waits for them, and re-layouts: 26.3 us -> none  [per_device(): lax.all_to_all(spectra, 'freq', split_axis=3, concat_axis=0, tiled=True)]
    unnamed x8 -> x16, local copies, waits for them, and re-layouts: 0.02 us -> 17.3 us
    ppermute x0 -> x7, starting transfers between devices: none -> 13.5 us  [per_device(): lax.ppermute(sent, 'freq', [(i, i ^ turn) for i in range(size)])]
    convert_element_type x0 -> x1, local copies, waits for them, and re-layouts: none -> 11.5 us  [per_device(): spectra = (spectra * (1.0 / math.sqrt(K))).astype(jnp.bfloat16).reshape(l...]
  transfers between devices with their start and end apart: 1 -> 8, of which waited for: 1 -> 5; matrix products, arithmetic and copies ran while one was open for 0% -> 2% of each run, Pallas kernels for 0% -> 0%
where the time goes in v1:
time: 625 us; the launch traced here: 623 us
  waiting for transfers between devices  365 us (58%)
  local copies, waits for them, and re-layouts  141 us (23%)
  other arithmetic  62.1 us (10%)
  matrix products  26.2 us (4%)
  between operations  14.8 us (2%)
  starting transfers between devices  13.5 us (2%)
    all_gather x1, waiting for transfers between devices, per_device(): gathered = lax.all_gather(turned, 'bl', axis=0, tiled=True)  240 us
    ppermute x7, waiting for transfers between devices, per_device(): lax.ppermute(sent, 'freq', [(i, i ^ turn) for i in range(size)])  125 us
    transpose x3, local copies, waits for them, and re-layouts, arrange(): jnp.transpose(panel, (3, 0, 2, 1))  39.2 us
    reshape x2, local copies, waits for them, and re-layouts, arrange(): jnp.transpose(panel, (3, 0, 2, 1))  28.2 us
    transpose x3, other arithmetic, arrange(): jnp.transpose(panel, (3, 0, 2, 1))  21.5 us
    convert_element_type x1, other arithmetic, per_device(): filtered = filtered.astype(jnp.bfloat16)  19.3 us
    unnamed x16, local copies, waits for them, and re-layouts  17.3 us
    dot_general x1, matrix products, correlate(): jnp.einsum('fps,fqs->fpq', left, right, preferred_element_type=jnp.float32)  15.2 us
  transfers between devices with their start and end apart: 8, of which 5 were waited for; matrix products, arithmetic and copies ran while one was open for 2% of the time, Pallas kernels for 0%

profile of v1, /device:TPU:0, one launch (start us, length us, event | category | flops | bytes accessed | tf_op | source)
XLA Modules:
  0.0 623.0 jit_solution(16674856525271084594)
XLA Ops:
  6.5 8.5 %negate_convert_fusion = (bf16[1024,512]{1,0:T(8,128)(2,1)S(1)}, bf16[1024,512]{1,0:T(8,128)(2,1)S(1)}) fusion(), kind=kLoop, calls=%fused_computation.24 | loop fusion | flops 8912896 | bytes 2097152 | tf_op jit(solution)/shard_map/convert.1
  15.1 9.2 %reshape.66 = bf16[32,131,1024]{2,1,0:T(8,128)(2,1)} reshape(bf16[32,134144]{1,0:T(8,128)(2,1)} %param.6) | data formatting | bytes 17170432 | tf_op jit(solution)/shard_map/reshape | solution.py:56
  24.4 19.3 %add_convert_fusion = bf16[32,128,1024]{2,1,0:T(8,128)(2,1)S(1)} fusion(bf16[32,131,1024]{2,1,0:T(8,128)(2,1)} %reshape.66, f32[1024]{0:T(1024)S(1)} %bitcast.77, f32[1024]{0:T(1024)S(1)} %bitcast.78, f32[1024]{0:T(1024)S(1)} %bitcast.76, f32[1024]{0:T(1024)S(1)} %bitcast.75), kind=kLoop, calls=%fused_computation.10 | loop fusion | flops 50331648 | bytes 41959424 | tf_op jit(solution)/shard_map/convert_element_type | solution.py:62
  43.6 11.0 %multiply_convert_fusion.1 = bf16[4096,1024]{1,0:T(8,128)(2,1)} fusion(bf16[4096,1024]{1,0:T(8,128)(2,1)S(1)} %bitcast.66, bf16[1024,512]{1,0:T(8,128)(2,1)S(1)} %get-tuple-element.28, bf16[1024,512]{1,0:T(8,128)(2,1)S(1)} %get-tuple-element.29), kind=kOutput, calls=%fused_computation.9 | convolution fusion | flops 8602517504 | bytes 18874368 | tf_op jit(solution)/shard_map/dot_general | solution.py:64
  54.6 11.5 %copy.29 = bf16[4096,1024]{0,1:T(8,128)(2,1)} copy(bf16[4096,1024]{1,0:T(8,128)(2,1)} %multiply_convert_fusion.1) | data formatting | bytes 16777216 | tf_op jit(solution)/shard_map/convert_element_type | solution.py:69
  66.1 9.6 %copy.43 = bf16[128,8,32,128]{3,2,1,0:T(8,128)(2,1)} copy(bf16[128,8,32,128]{3,1,2,0:T(8,128)(2,1)} %bitcast.65) | data formatting | bytes 16777216
  94.2 13.2 %collective-permute-done = bf16[32,128,2,64]{1,3,2,0:T(8,128)(2,1)S(1)} collective-permute-done((bf16[32,128,2,64]{1,3,2,0:T(8,128)(2,1)S(1)}, bf16[32,128,2,64]{1,3,2,0:T(8,128)(2,1)S(1)}, u32[]{:S(2)}, u32[]{:S(2)}) %collective-permute-start) | collective-permute-done | bytes 1048608 | tf_op jit(solution)/shard_map/ppermute | solution.py:77
  112.3 42.0 %collective-permute-done.1 = bf16[32,128,2,64]{1,3,2,0:T(8,128)(2,1)S(1)} collective-permute-done((bf16[32,128,2,64]{1,3,2,0:T(8,128)(2,1)S(1)}, bf16[32,128,2,64]{1,3,2,0:T(8,128)(2,1)S(1)}, u32[]{:S(2)}, u32[]{:S(2)}) %collective-permute-start.1) | collective-permute-done | bytes 1048608 | tf_op jit(solution)/shard_map/ppermute | solution.py:77
  155.9 18.4 %collective-permute-done.2 = bf16[32,128,2,64]{1,3,2,0:T(8,128)(2,1)S(1)} collective-permute-done((bf16[32,128,2,64]{1,3,2,0:T(8,128)(2,1)S(1)}, bf16[32,128,2,64]{1,3,2,0:T(8,128)(2,1)S(1)}, u32[]{:S(2)}, u32[]{:S(2)}) %collective-permute-start.2) | collective-permute-done | bytes 1048608 | tf_op jit(solution)/shard_map/ppermute | solution.py:77
  176.5 51.5 %collective-permute-done.4 = bf16[32,128,2,64]{1,3,2,0:T(8,128)(2,1)S(1)} collective-permute-done((bf16[32,128,2,64]{1,3,2,0:T(8,128)(2,1)S(1)}, bf16[32,128,2,64]{1,3,2,0:T(8,128)(2,1)S(1)}, u32[]{:S(2)}, u32[]{:S(2)}) %collective-permute-start.4) | collective-permute-done | bytes 1048608 | tf_op jit(solution)/shard_map/ppermute | solution.py:77
  231.1 8.1 %gather_fusion = bf16[8,32,128,2,64]{2,4,3,1,0:T(8,128)(2,1)} fusion(bf16[8,32,128,2,64]{2,4,3,1,0:T(8,128)(2,1)} %bitcast_dynamic-update-slice_fusion, s32[1024]{0:T(1024)S(1)} %pad_clamp_fusion.2), kind=kCustom, calls=%fused_computation.2 | custom fusion | bytes 16777248 | tf_op jit(solution)/shard_map/gather | solution.py:78
  241.2 239.9 %all-gather.2.cloned.1.call-done = bf16[1024,128,2,64]{1,3,2,0:T(8,128)(2,1)} async-done(((bf16[256,128,2,64]{1,3,2,0:T(8,128)(2,1)}), bf16[1024,128,2,64]{1,3,2,0:T(8,128)(2,1)}) %all-gather.2.cloned.1.call-update) | async-done | bytes 33554448 | tf_op jit(solution)/shard_map/all_gather | solution.py:80
  481.1 9.1 %gather_fusion.2 = bf16[256,128,2,64]{1,3,2,0:T(8,128)(2,1)} fusion(bf16[1024,128,2,64]{1,3,2,0:T(8,128)(2,1)} %all-gather.2.cloned.1.call-done, s32[1024]{0:T(1024)S(1)} %get-tuple-element.30), kind=kCustom, calls=%fused_computation.1.clone | custom fusion | bytes 16778240 | tf_op jit(solution)/shard_map/jit(_take)/gather | solution.py:48
  490.2 7.4 %broadcast_select_fusion = bf16[256,128,2,64]{1,3,2,0:T(8,128)(2,1)} fusion(bf16[256,128,2,64]{1,3,2,0:T(8,128)(2,1)} %gather_fusion.2, pred[256]{0:T(512)(128)(4,1)S(1)} %get-tuple-element.6), kind=kLoop, calls=%fused_computation.13 | loop fusion | flops 4194304 | bytes 16777472 | tf_op jit(solution)/shard_map/jit(_take)/select_n | solution.py:48
  497.6 7.4 %fusion.23 = bf16[64,256,2,128]{3,0,2,1:T(8,128)(2,1)} fusion(bf16[256,128,2,64]{1,3,2,0:T(8,128)(2,1)} %gather_fusion.2, pred[256]{0:T(512)(128)(4,1)S(1)} %get-tuple-element.6), kind=kLoop, calls=%fused_computation.66 | loop fusion | flops 4194304 | bytes 16777472 | tf_op jit(solution)/shard_map/transpose | solution.py:36
  505.1 9.1 %gather_fusion.1 = bf16[256,128,2,64]{1,3,2,0:T(8,128)(2,1)} fusion(bf16[1024,128,2,64]{1,3,2,0:T(8,128)(2,1)} %all-gather.2.cloned.1.call-done, s32[1024]{0:T(1024)S(1)} %get-tuple-element.31), kind=kCustom, calls=%fused_computation.clone | custom fusion | bytes 16778240 | tf_op jit(solution)/shard_map/jit(_take)/gather | solution.py:47
  514.2 7.6 %select_bitcast_fusion = bf16[64,256,2,128]{3,0,2,1:T(8,128)(2,1)} fusion(bf16[256,128,2,64]{1,3,2,0:T(8,128)(2,1)} %gather_fusion.1, pred[256]{0:T(512)(128)(4,1)S(1)} %get-tuple-element.24), kind=kLoop, calls=%fused_computation.12 | loop fusion | flops 4194304 | bytes 16777472 | tf_op jit(solution)/shard_map/transpose | solution.py:36
  521.8 12.9 %copy.38 = bf16[64,256,2,128]{1,3,2,0:T(8,128)(2,1)} copy(bf16[64,256,2,128]{3,0,2,1:T(8,128)(2,1)} %select_bitcast_fusion) | data formatting | bytes 16777216 | tf_op jit(solution)/shard_map/transpose | solution.py:36
  539.9 6.5 %maximum_bitcast_fusion = bf16[64,256,2,128]{3,0,2,1:T(8,128)(2,1)} fusion(bf16[256,128,1,64]{1,3,2,0:T(8,128)(2,1)} %get-tuple-element.11, bf16[256,128,1,64]{1,3,2,0:T(8,128)(2,1)S(1)} %get-tuple-element.10), kind=kLoop, calls=%fused_computation.11 | loop fusion | flops 4194304 | bytes 16777216 | tf_op jit(solution)/shard_map/transpose | solution.py:36
  546.4 13.2 %copy.40 = bf16[64,256,2,128]{3,2,1,0:T(2,128)(2,1)} copy(bf16[64,256,2,128]{3,0,2,1:T(8,128)(2,1)} %maximum_bitcast_fusion) | data formatting | bytes 16777216 | tf_op jit(solution)/shard_map/transpose | solution.py:36
  559.6 14.1 %reshape.71 = bf16[64,256,256]{2,1,0:T(8,128)(2,1)} reshape(bf16[64,256,2,128]{3,2,1,0:T(2,128)(2,1)} %copy.40) | data formatting | bytes 16777216 | tf_op jit(solution)/shard_map/reshape | solution.py:36
  573.7 13.2 %copy.39 = bf16[64,256,2,128]{3,2,1,0:T(2,128)(2,1)} copy(bf16[64,256,2,128]{3,0,2,1:T(8,128)(2,1)} %fusion.23) | data formatting | bytes 16777216 | tf_op jit(solution)/shard_map/transpose | solution.py:36
  586.9 14.1 %reshape.70 = bf16[64,256,256]{2,1,0:T(8,128)(2,1)} reshape(bf16[64,256,2,128]{3,2,1,0:T(2,128)(2,1)} %copy.39) | data formatting | bytes 16777216 | tf_op jit(solution)/shard_map/reshape | solution.py:36
  600.9 15.2 %fusion = bf16[1,64,256,512]{3,2,1,0:T(8,128)(2,1)} fusion(bf16[64,256,256]{1,2,0:T(8,128)(2,1)} %bitcast.67, bf16[64,256,256]{2,1,0:T(8,128)(2,1)} %reshape.71, bf16[64,256,256]{2,1,0:T(8,128)(2,1)} %reshape.70), kind=kOutput, calls=%fused_computation.4 | convolution fusion | flops 4345298944 | bytes 41943040 | tf_op jit(solution)/shard_map/fps,fqs->fpq/dot_general | solution.py:51
  (44 shorter events, 36.2 us)
Async XLA Ops:
  6.5 232.6 %copy-start = (s32[4,2]{0,1:T(2,128)S(1)}, s32[4,2]{0,1:T(2,128)}, u32[]{:S(2)}) copy-start(s32[4,2]{0,1:T(2,128)} %param.9) | copy-start | bytes 100
  6.5 474.6 %all-gather.2.cloned.1.call-start = ((), (), s32[]{:S(2)}) async-start(), calls=%async_computation | async-start | bytes 41943040 | tf_op jit(solution)/shard_map/all_gather | solution.py:80
  15.1 9.2 %copy-start.2 = (f32[4,1024]{1,0:T(4,128)S(1)}, f32[4,1024]{1,0:T(4,128)}, u32[]{:S(2)}) copy-start(f32[4,1024]{1,0:T(4,128)} %param.7) | copy-start | bytes 49156
  81.2 26.2 %collective-permute-start = (bf16[32,128,2,64]{1,3,2,0:T(8,128)(2,1)S(1)}, bf16[32,128,2,64]{1,3,2,0:T(8,128)(2,1)S(1)}, u32[]{:S(2)}, u32[]{:S(2)}) collective-permute-start(bf16[32,128,2,64]{1,3,2,0:T(8,128)(2,1)S(1)} %bitcast.74), channel_id=1, source_target_pairs={{0,4},{4,0},{8,12},{12,8},{16,20},{20,16},{24,28},{28,24},{1,5},{5... | collective-permute-start | bytes 3145736 | tf_op jit(solution)/shard_map/ppermute | solution.py:77
  84.6 69.7 %collective-permute-start.1 = (bf16[32,128,2,64]{1,3,2,0:T(8,128)(2,1)S(1)}, bf16[32,128,2,64]{1,3,2,0:T(8,128)(2,1)S(1)}, u32[]{:S(2)}, u32[]{:S(2)}) collective-permute-start(bf16[32,128,2,64]{1,3,2,0:T(8,128)(2,1)S(1)} %bitcast.73), channel_id=1, source_target_pairs={{0,8},{4,12},{8,0},{12,4},{16,24},{20,28},{24,16},{28,20},{1,9},{5... | collective-permute-start | bytes 3145736 | tf_op jit(solution)/shard_map/ppermute | solution.py:77
  86.7 87.7 %collective-permute-start.2 = (bf16[32,128,2,64]{1,3,2,0:T(8,128)(2,1)S(1)}, bf16[32,128,2,64]{1,3,2,0:T(8,128)(2,1)S(1)}, u32[]{:S(2)}, u32[]{:S(2)}) collective-permute-start(bf16[32,128,2,64]{1,3,2,0:T(8,128)(2,1)S(1)} %bitcast.72), channel_id=1, source_target_pairs={{0,12},{4,8},{8,4},{12,0},{16,28},{20,24},{24,20},{28,16},{1,13},{... | collective-permute-start | bytes 3145736 | tf_op jit(solution)/shard_map/ppermute | solution.py:77
  87.2 88.2 %collective-permute-start.3 = (bf16[32,128,2,64]{1,3,2,0:T(8,128)(2,1)S(1)}, bf16[32,128,2,64]{1,3,2,0:T(8,128)(2,1)S(1)}, u32[]{:S(2)}, u32[]{:S(2)}) collective-permute-start(bf16[32,128,2,64]{1,3,2,0:T(8,128)(2,1)S(1)} %bitcast.71), channel_id=1, source_target_pairs={{0,16},{4,20},{8,24},{12,28},{16,0},{20,4},{24,8},{28,12},{1,17},{... | collective-permute-start | bytes 3145736 | tf_op jit(solution)/shard_map/ppermute | solution.py:77
  90.6 137.3 %collective-permute-start.4 = (bf16[32,128,2,64]{1,3,2,0:T(8,128)(2,1)S(1)}, bf16[32,128,2,64]{1,3,2,0:T(8,128)(2,1)S(1)}, u32[]{:S(2)}, u32[]{:S(2)}) collective-permute-start(bf16[32,128,2,64]{1,3,2,0:T(8,128)(2,1)S(1)} %bitcast.70), channel_id=1, source_target_pairs={{0,20},{4,16},{8,28},{12,24},{16,4},{20,0},{24,12},{28,8},{1,21},{... | collective-permute-start | bytes 3145736 | tf_op jit(solution)/shard_map/ppermute | solution.py:77
  107.4 121.6 %collective-permute-start.5 = (bf16[32,128,2,64]{1,3,2,0:T(8,128)(2,1)S(1)}, bf16[32,128,2,64]{1,3,2,0:T(8,128)(2,1)S(1)}, u32[]{:S(2)}, u32[]{:S(2)}) collective-permute-start(bf16[32,128,2,64]{1,3,2,0:T(8,128)(2,1)S(1)} %bitcast.69), channel_id=1, source_target_pairs={{0,24},{4,28},{8,16},{12,20},{16,8},{20,12},{24,0},{28,4},{1,25},{... | collective-permute-start | bytes 3145736 | tf_op jit(solution)/shard_map/ppermute | solution.py:77
  154.3 75.7 %collective-permute-start.6 = (bf16[32,128,2,64]{1,3,2,0:T(8,128)(2,1)S(1)}, bf16[32,128,2,64]{1,3,2,0:T(8,128)(2,1)S(1)}, u32[]{:S(2)}, u32[]{:S(2)}) collective-permute-start(bf16[32,128,2,64]{1,3,2,0:T(8,128)(2,1)S(1)} %bitcast.68), channel_id=1, source_target_pairs={{0,28},{4,24},{8,20},{12,16},{16,12},{20,8},{24,4},{28,0},{1,29},{... | collective-permute-start | bytes 3145736 | tf_op jit(solution)/shard_map/ppermute | solution.py:77
  239.1 2.0 copy-start.3
  600.9 15.2 %copy-start.1 = (s32[4,2]{0,1:T(2,128)S(1)}, s32[4,2]{0,1:T(2,128)}, u32[]{:S(2)}) copy-start(s32[4,2]{0,1:T(2,128)} %param.9) | copy-start | bytes 100
Sparse Core Ops, SparseCore 0:
  239.3 241.7 all-gather.1
